TPU v7x, 32 devices: a whole 2x2x4 slice. The times are simulated.
32 devices in a mesh: frag: 2 (over x), aux: 16 (over z, y, core).
Axes of the slice: x: 2, y: 2, z: 4, core: 2. Of those that a mesh axis runs over, the one named last changes fastest.
Arguments:
- three_index: bfloat16 [512, 8, 128, 128], P(('frag', 'aux')), parts along dimension 0, may hold values from -0.125 to 0.125
- slab_blocks: int32 [512], P(('frag', 'aux')), parts along dimension 0, may hold values from 0 to 255
- slab_count: int32 [32], P(('frag', 'aux')), parts along dimension 0, may hold values from 1 to 16, 128 in all
- pair_mask: int32 [32, 16], P('frag'), parts along dimension 0, may hold values 0 or 1
- coeffs: bfloat16 [4096, 200], P(('frag', 'aux')), parts along dimension 0, may hold values from -1 to 1
Outputs:
- exchange: float32 [4096, 2048], P(('frag', 'aux')), parts along dimension 0
There are 2 independent parts, one for each index of `frag`. A program takes and returns all parts, laid end to end along the dimension named above; each array names one. Nothing has to cross between parts.
Inputs may be any that keep to these rules, and one draw needn't show every extreme that they name: `slab_count`: each slab has 1 to 16 live slots; some slab has exactly 16; within each fragment the counts sum to 128. `slab_blocks`: slots past a slab's count carry values that do not count; a block pair may stand in several slots of a slab.
All inputs are finite; a program needn't handle non-finite values. No bound on the sum of `slab_count` on one device may be relied on, other than what follows from the above.
Results may differ from a plain program's by a relative error of at most 0.0012.
Values may be sent and summed in bfloat16 or wider, within the bound.
A program may use at most 128 MiB of HBM per device.

v0:
```python
import functools

import jax
import jax.numpy as jnp
from jax import lax
from jax.experimental import pallas as pl
from jax.experimental.pallas import tpu as pltpu
from jax.sharding import PartitionSpec as P

MESH = pl.DeviceIdType.MESH
VMEM_BYTES = 56 * 1024 * 1024
TOP = 32000.0
TINY = 1e-37
LANES = 256


def flip(value, bits):
    return sum(((value >> j) & 1) << (bits - 1 - j) for j in range(bits))


def partners_of(me, stages):
    return [me + (1 << k) * (1 - 2 * ((me // (1 << k)) % 2)) for k in range(stages)]


def gather_kernel(c_ref, g_ref, send_sem, recv_sem, *, n):
    stages = n.bit_length() - 1
    me = lax.axis_index("aux")
    partner = partners_of(me, stages)
    barrier = pltpu.get_barrier_semaphore()
    for peer in partner:
        pl.semaphore_signal(barrier, inc=1, device_id={"aux": peer}, device_id_type=MESH)
    g_ref[me] = jnp.zeros(g_ref.shape[1:], g_ref.dtype)
    g_ref[me, :, 0:c_ref.shape[0]] = c_ref[...].T
    pl.semaphore_wait(barrier, stages)

    def copy(x, k):
        unit = me + sum(partner[j] - me for j in range(stages) if (x >> j) & 1)
        return pltpu.make_async_remote_copy(
            src_ref=g_ref.at[unit], dst_ref=g_ref.at[unit], send_sem=send_sem.at[x, k], recv_sem=recv_sem.at[x ^ (1 << k)],
            device_id={"aux": partner[k]}, device_id_type=MESH)

    started = []
    for x in sorted(range(n), key=lambda x: (x.bit_count(), -x)):
        low = stages if x == 0 else (x & -x).bit_length() - 1
        if x:
            copy(x ^ (1 << low), low).wait_recv()
        for k in reversed(range(low)):
            started.append(copy(x, k))
            started[-1].start()
    for one in started:
        one.wait_send()


def slab_kernel(blocks, count, mask, t_ref, c_ref, q_ref, m_ref, total, factor, seen, *, slots, width, split):
    g = pl.program_id(0)
    nb, size, _ = c_ref.shape
    aux = t_ref.shape[1]
    chunks, cw = q_ref.shape[0], q_ref.shape[4]
    group = max(d for d in range(1, 5) if width % d == 0)
    per = cw // size
    rows = size // split

    @pl.when(g == 0)
    def _():
        for r in range(nb):
            seen[r] = 0
        m_ref[...] = jnp.zeros_like(m_ref)

    @pl.when(g < slots)
    def _():
        pair = blocks[g]
        row, col = pair // nb, pair % nb
        live = (g < count[0]) & (mask[row, col] == 1)

        @pl.when(live)
        def _():
            part = jnp.dot(t_ref[0].reshape(aux * size, size), c_ref[col], preferred_element_type=jnp.float32)
            before = seen[row]

            @pl.when(before == 0)
            def _():
                total[row] = part

            @pl.when(before != 0)
            def _():
                total[row] += part

            seen[row] = 1

    @pl.when(g == slots)
    def _():
        @pl.loop(0, nb)
        def _(r):
            @pl.when(seen[r] != 0)
            def _():
                for p in range(aux):
                    factor[r, :, p * LANES:(p + 1) * LANES] = total[r, p * size:(p + 1) * size].astype(jnp.bfloat16)

            @pl.when(seen[r] == 0)
            def _():
                factor[r] = jnp.zeros(factor.shape[1:], factor.dtype)

            @pl.when(r < width - 1)
            def _():
                factor[nb + r] = factor[r]

    @pl.when(g >= slots)
    def _():
        r = g - slots

        @pl.when(seen[r] != 0)
        def _():
            for d in range(0, width, group):
                right = factor[pl.ds(r + d, group)].reshape(group * size, factor.shape[2])
                value = lax.dot_general(factor[r], right, (((1,), (1,)), ((), ())), preferred_element_type=jnp.float32)
                for h in range(split):
                    for i in range(0, group, per):
                        q_ref[(d + i) // per, flip(h, split.bit_length() - 1), 0] = value[h * rows:(h + 1) * rows, i * size:(i + per) * size]
                if d == 0:
                    m_ref[...] = jnp.maximum(m_ref[...], jnp.max(jnp.abs(value[:, :size])))

        @pl.when(seen[r] == 0)
        def _():
            q_ref[...] = jnp.zeros_like(q_ref)


def encode(value, inverse):
    root = jnp.sqrt(jnp.abs(value) * inverse) * TOP + 0.5
    return jnp.where(value < 0, -root, root).astype(jnp.int16)


def decode(code, scale):
    value = code.astype(jnp.float32)
    return value * jnp.abs(value) * scale


def reduce_kernel(q_ref, m_ref, out_ref, acc, snd, rcv, s_m, r_m, m_snd, m_rcv, send_sem, recv_sem, sm_send, sm_recv, mir_send, mir_recv, *, n, nb, width, mirrored):
    chunks, _, rows, cw = q_ref.shape
    size = out_ref.shape[1] // nb
    per = width // chunks
    stages = n.bit_length() - 1
    me = lax.axis_index("aux")
    r = me // (n // nb)
    bit = [(me // (1 << k)) % 2 for k in range(stages)]
    partner = partners_of(me, stages)
    counts = [n >> (k + 1) for k in range(stages)]
    starts = [n - (n >> k) for k in range(stages)]
    steps = [min(4, count) for count in counts]
    mirror = list(range(1, width - 1)) if mirrored else []

    barrier = pltpu.get_barrier_semaphore()
    if mirrored:
        peers = [lax.rem(me + d, n) for d in range(1, n)]
    else:
        peers = partner
    for peer in peers:
        pl.semaphore_signal(barrier, inc=1, device_id={"aux": peer}, device_id_type=MESH)
    pl.semaphore_wait(barrier, len(peers))

    def scale_copy(k):
        return pltpu.make_async_remote_copy(
            src_ref=s_m.at[k], dst_ref=r_m.at[k], send_sem=sm_send.at[k], recv_sem=sm_recv.at[k],
            device_id={"aux": partner[k]}, device_id_type=MESH)

    def data_copy(k, c):
        span = pl.ds(starts[k], counts[k])
        return pltpu.make_async_remote_copy(
            src_ref=snd.at[c, span], dst_ref=rcv.at[c, span], send_sem=send_sem.at[k, c], recv_sem=recv_sem.at[k, c],
            device_id={"aux": partner[k]}, device_id_type=MESH)

    def mirror_copy(d):
        return pltpu.make_async_remote_copy(
            src_ref=m_snd.at[d], dst_ref=m_rcv.at[d], send_sem=mir_send.at[d], recv_sem=mir_recv.at[d],
            device_id={"aux": lax.rem(me + d, n)}, device_id_type=MESH)

    def place(block, value):
        out_ref[:, pl.ds(pl.multiple_of(block * size, size), size)] = value

    def before(k, c, j):
        return q_ref[c, pl.ds(bit[0] * counts[0] + j, steps[k])] if k == 1 else acc[c, pl.ds(j, steps[k])]

    def event(k, c):
        if k == 0:
            if c == 0:
                s_m[0] = jnp.maximum(m_ref[...], TINY)
                scale_copy(0).start()
            inverse = 1.0 / s_m[0, 0:1]

            @pl.loop(0, counts[0], step=steps[0])
            def _(j):
                snd[c, pl.ds(j, steps[0])] = encode(q_ref[c, pl.ds((1 - bit[0]) * counts[0] + j, steps[0])], inverse)

            data_copy(0, c).start()
            return
        if c == 0:
            scale_copy(k - 1).wait_recv()
            if k < stages:
                s_m[k] = s_m[k - 1] + r_m[k - 1]
                scale_copy(k).start()
        back = r_m[k - 1, 0:1] * (1.0 / (TOP * TOP))
        data_copy(k - 1, c).wait_recv()
        if k < stages:
            inverse = 1.0 / s_m[k, 0:1]

            @pl.loop(0, counts[k], step=steps[k])
            def _(j):
                i = (1 - bit[k]) * counts[k] + j
                value = before(k, c, i) + decode(rcv[c, pl.ds(starts[k - 1] + i, steps[k])], back)
                snd[c, pl.ds(starts[k] + j, steps[k])] = encode(value, inverse)

            data_copy(k, c).start()

            @pl.loop(0, counts[k], step=steps[k])
            def _(j):
                i = bit[k] * counts[k] + j
                acc[c, pl.ds(j, steps[k])] = before(k, c, i) + decode(rcv[c, pl.ds(starts[k - 1] + i, steps[k])], back)

            return
        value = acc[c, 0] + decode(rcv[c, starts[k - 1]], back)
        for i in range(per):
            d = c * per + i
            block = value[:, i * size:(i + 1) * size]
            if d in mirror:
                m_snd[d] = block.T
                mirror_copy(d).start()
            place(lax.rem(r + d, nb), block)

    def due(k, c):
        return (0.5 * c + 1.7 * k if k < 2 else 3.2 + 2.6 * (c + 1) + 2.5 * (k - 2), k, c)

    for k, c in sorted(((k, c) for k in range(stages + 1) for c in range(chunks)), key=lambda e: due(*e)):
        event(k, c)
    for d in mirror:
        mirror_copy(d).wait_recv()
        place(lax.rem(r + nb - d, nb), m_rcv[d])
    for k in range(stages):
        scale_copy(k).wait_send()
        for c in range(chunks):
            data_copy(k, c).wait_send()
    for d in mirror:
        mirror_copy(d).wait_send()


def per_device(n, three_index, slab_blocks, slab_count, pair_mask, coeffs):
    slots, aux, size, _ = three_index.shape
    nb = pair_mask.shape[0]
    mirrored = n == nb
    split = n // nb
    width = nb // 2 + 1 if mirrored else nb
    per = 1 if mirrored else 2
    chunks, cw, rows = width // per, per * size, size // split
    bits = nb.bit_length() - 1
    stages = n.bit_length() - 1
    gathered = pl.pallas_call(
        functools.partial(gather_kernel, n=n),
        out_shape=jax.ShapeDtypeStruct((n, rows, LANES), coeffs.dtype),
        in_specs=[pl.BlockSpec(memory_space=pltpu.VMEM)],
        out_specs=pl.BlockSpec(memory_space=pltpu.VMEM),
        scratch_shapes=[pltpu.SemaphoreType.DMA((n, stages)), pltpu.SemaphoreType.DMA((n,))],
        compiler_params=pltpu.CompilerParams(collective_id=1, has_side_effects=True, vmem_limit_bytes=VMEM_BYTES),
    )(coeffs.T).reshape(nb, size, LANES)

    q, m = pl.pallas_call(
        functools.partial(slab_kernel, slots=slots, width=width, split=split),
        grid_spec=pltpu.PrefetchScalarGridSpec(
            num_scalar_prefetch=3,
            grid=(slots + nb,),
            in_specs=[
                pl.BlockSpec((1, aux, size, size), lambda g, *_: (jnp.minimum(g, slots - 1), 0, 0, 0)),
                pl.BlockSpec((nb, size, LANES), lambda g, *_: (0, 0, 0)),
            ],
            out_specs=[
                pl.BlockSpec((chunks, split, 1, rows, cw), lambda g, *_: (0, 0, flip(jnp.maximum(g - slots, 0), bits), 0, 0)),
                pl.BlockSpec((8, cw), lambda g, *_: (0, 0)),
            ],
            scratch_shapes=[
                pltpu.VMEM((nb, aux * size, LANES), jnp.float32),
                pltpu.VMEM((nb + width - 1, size, aux * LANES), jnp.bfloat16),
                pltpu.SMEM((nb,), jnp.int32),
            ],
        ),
        out_shape=[
            jax.ShapeDtypeStruct((chunks, split, nb, rows, cw), jnp.float32),
            jax.ShapeDtypeStruct((8, cw), jnp.float32),
        ],
        compiler_params=pltpu.CompilerParams(vmem_limit_bytes=VMEM_BYTES, dimension_semantics=("arbitrary",)),
    )(slab_blocks, slab_count, pair_mask, three_index, gathered)

    return pl.pallas_call(
        functools.partial(reduce_kernel, n=n, nb=nb, width=width, mirrored=mirrored),
        out_shape=jax.ShapeDtypeStruct((rows, nb * size), jnp.float32),
        in_specs=[pl.BlockSpec(memory_space=pltpu.VMEM)] * 2,
        out_specs=pl.BlockSpec(memory_space=pltpu.VMEM),
        scratch_shapes=[
            pltpu.VMEM((chunks, n // 4, rows, cw), jnp.float32),
            pltpu.VMEM((chunks, n, rows, cw), jnp.int16),
            pltpu.VMEM((chunks, n, rows, cw), jnp.int16),
            pltpu.VMEM((stages, 8, cw), jnp.float32),
            pltpu.VMEM((stages, 8, cw), jnp.float32),
            pltpu.VMEM((width, size, size), jnp.float32),
            pltpu.VMEM((width, size, size), jnp.float32),
            pltpu.SemaphoreType.DMA((stages, chunks)),
            pltpu.SemaphoreType.DMA((stages, chunks)),
            pltpu.SemaphoreType.DMA((stages,)),
            pltpu.SemaphoreType.DMA((stages,)),
            pltpu.SemaphoreType.DMA((width,)),
            pltpu.SemaphoreType.DMA((width,)),
        ],
        compiler_params=pltpu.CompilerParams(collective_id=0, has_side_effects=True, vmem_limit_bytes=VMEM_BYTES),
    )(q.reshape(chunks, n, rows, cw), m)


def solution(mesh):
    return jax.shard_map(
        functools.partial(per_device, mesh.shape["aux"]),
        mesh=mesh,
        in_specs=(
            P(("frag", "aux"), None, None, None),
            P(("frag", "aux")),
            P(("frag", "aux")),
            P("frag", None),
            P(("frag", "aux"), None),
        ),
        out_specs=P(("frag", "aux"), None),
        check_vma=False,
    )
```

profile of v0, /device:TPU:1, one launch (start us, length us, event | category | flops | bytes accessed | tf_op | source)
XLA Modules:
  0.0 114.2 jit_solution(4069183668337949053)
XLA Ops:
  0.7 18.4 %shard_map.55.c_ref = bf16[16,128,256]{2,1,0:T(8,128)(2,1)} custom-call(bf16[200,128]{1,0:T(8,128)(2,1)} %bitcast.3), custom_call_target="tpu_custom_call" | custom-call | tf_op jit(solution)/shard_map/pallas_call | solution.py:254
  19.0 19.3 %shard_map.56 = (f32[9,1,16,128,128]{4,3,2,1,0:T(8,128)}, f32[8,128]{1,0:T(8,128)}) custom-call(s32[16]{0:T(128)} %blocks.1, s32[1]{0:T(128)S(6)} %copy.7.count, s32[16,16]{1,0:T(8,128)} %mask.1, bf16[16,8,128,128]{3,2,1,0:T(8,128)(2,1)} %t_ref.1, bf16[16,128,256]{2,1,0:T(8,128)(2,1)} %shard_map.55.c_ref), custom_call_target="tpu_custom_call" | custom-call | tf_op jit(solution)/shard_map/pallas_call | solution.py:263
  38.3 73.7 %shard_map.57 = f32[128,2048]{1,0:T(8,128)} custom-call(f32[9,16,128,128]{3,2,1,0:T(8,128)} %bitcast.2, f32[8,128]{1,0:T(8,128)} %get-tuple-element.8.m_ref), custom_call_target="tpu_custom_call" | custom-call | tf_op jit(solution)/shard_map/pallas_call | solution.py:289
  111.9 2.3 %copy.8 = f32[128,2048]{1,0:T(8,128)} copy(f32[128,2048]{1,0:T(8,128)} %shard_map.57) | data formatting | bytes 2097152
where the time goes:
time: 114 us
  Pallas kernels  111 us (97%)
  local copies, waits for them, and re-layouts  2.3 us (2%)
    pallas_call x1, Pallas kernels, per_device(): pl.pallas_call(functools.partial(reduce_kernel, n=n, nb=nb, width=width,...  73.7 us
    pallas_call x1, Pallas kernels, per_device(): pl.pallas_call(functools.partial(slab_kernel, slots=slots, width=width, s...  19.3 us
    pallas_call x1, Pallas kernels, per_device(): pl.pallas_call(functools.partial(gather_kernel, n=n), out_shape=jax.Shape...  18.4 us
    unnamed x1, local copies, waits for them, and re-layouts  2.3 us

commit v1 on v0

--- a/solution.py
+++ b/solution.py
@@ -51,50 +51,53 @@
         one.wait_send()
 
 
-def slab_kernel(blocks, count, mask, t_ref, c_ref, q_ref, m_ref, total, factor, seen, *, slots, width, split):
+def slab_kernel(blocks, count, mask, t_ref, c_ref, send_ref, keep_ref, m_ref, total, factor, seen, *, width, split):
     g = pl.program_id(0)
     nb, size, _ = c_ref.shape
-    aux = t_ref.shape[1]
-    chunks, cw = q_ref.shape[0], q_ref.shape[4]
+    slots, aux = t_ref.shape[:2]
+    chunks, parts, batch, rows, cw = send_ref.shape
     group = max(d for d in range(1, 5) if width % d == 0)
     per = cw // size
-    rows = size // split
+    mine = lax.axis_index("aux") % 2
 
     @pl.when(g == 0)
     def _():
         for r in range(nb):
             seen[r] = 0
-        m_ref[...] = jnp.zeros_like(m_ref)
-
-    @pl.when(g < slots)
-    def _():
-        pair = blocks[g]
-        row, col = pair // nb, pair % nb
-        live = (g < count[0]) & (mask[row, col] == 1)
-
-        @pl.when(live)
-        def _():
-            part = jnp.dot(t_ref[0].reshape(aux * size, size), c_ref[col], preferred_element_type=jnp.float32)
-            before = seen[row]
-
-            @pl.when(before == 0)
-            def _():
-                total[row] = part
-
-            @pl.when(before != 0)
-            def _():
-                total[row] += part
-
-            seen[row] = 1
-
-    @pl.when(g == slots)
-    def _():
+        m_ref[...] = jnp.full(m_ref.shape, TINY, m_ref.dtype)
+
+        @pl.loop(0, slots)
+        def _(q):
+            pair = blocks[q]
+            row, col = pair // nb, pair % nb
+            live = (q < count[0]) & (mask[row, col] == 1)
+
+            @pl.when(live)
+            def _():
+                part = jnp.dot(t_ref[q].reshape(aux * size, size), c_ref[col], preferred_element_type=jnp.float32)
+                before = seen[row]
+
+                @pl.when(before == 0)
+                def _():
+                    total[row] = part
+
+                @pl.when(before != 0)
+                def _():
+                    total[row] += part
+
+                seen[row] = 1
+
         @pl.loop(0, nb)
         def _(r):
             @pl.when(seen[r] != 0)
             def _():
+                squares = jnp.zeros((size, LANES), jnp.float32)
                 for p in range(aux):
-                    factor[r, :, p * LANES:(p + 1) * LANES] = total[r, p * size:(p + 1) * size].astype(jnp.bfloat16)
+                    rounded = total[r, p * size:(p + 1) * size].astype(jnp.bfloat16)
+                    factor[r, :, p * LANES:(p + 1) * LANES] = rounded
+                    wide = rounded.astype(jnp.float32)
+                    squares += wide * wide
+                m_ref[...] = jnp.maximum(m_ref[...], jnp.max(jnp.sum(squares, axis=1)))
 
             @pl.when(seen[r] == 0)
             def _():
@@ -104,24 +107,41 @@
             def _():
                 factor[nb + r] = factor[r]
 
-    @pl.when(g >= slots)
-    def _():
-        r = g - slots
-
-        @pl.when(seen[r] != 0)
+    def fill(out_ref, first, odd, convert):
+        @pl.loop(0, batch)
+        def _(j):
+            r = flip(first + j, nb.bit_length() - 1)
+
+            @pl.when(seen[r] != 0)
+            def _():
+                for h in range(parts):
+                    left = factor[r] if split == 1 else factor[r, pl.ds(pl.multiple_of((2 * h + odd) * rows, rows), rows)]
+                    for d in range(0, width, group):
+                        right = factor[pl.ds(r + d, group)].reshape(group * size, factor.shape[2])
+                        value = convert(lax.dot_general(left, right, (((1,), (1,)), ((), ())), preferred_element_type=jnp.float32))
+                        for i in range(0, group, per):
+                            out_ref[(d + i) // per, flip(h, parts.bit_length() - 1), j] = value[:, i * size:(i + per) * size]
+
+            @pl.when(seen[r] == 0)
+            def _():
+                for c in range(chunks):
+                    for h in range(parts):
+                        out_ref[c, h, j] = jnp.zeros((rows, cw), out_ref.dtype)
+
+    inverse = 1.0 / m_ref[0:1, 0:1]
+    if split == 1:
+        half = nb // 2
+
+        @pl.when(g * batch < half)
         def _():
-            for d in range(0, width, group):
-                right = factor[pl.ds(r + d, group)].reshape(group * size, factor.shape[2])
-                value = lax.dot_general(factor[r], right, (((1,), (1,)), ((), ())), preferred_element_type=jnp.float32)
-                for h in range(split):
-                    for i in range(0, group, per):
-                        q_ref[(d + i) // per, flip(h, split.bit_length() - 1), 0] = value[h * rows:(h + 1) * rows, i * size:(i + per) * size]
-                if d == 0:
-                    m_ref[...] = jnp.maximum(m_ref[...], jnp.max(jnp.abs(value[:, :size])))
-
-        @pl.when(seen[r] == 0)
+            fill(send_ref, (1 - mine) * half + g * batch, 0, lambda value: encode(value, inverse))
+
+        @pl.when(g * batch >= half)
         def _():
-            q_ref[...] = jnp.zeros_like(q_ref)
+            fill(keep_ref, mine * half + g * batch - half, 0, lambda value: value)
+    else:
+        fill(send_ref, g * batch, 1 - mine, lambda value: encode(value, inverse))
+        fill(keep_ref, g * batch, mine, lambda value: value)
 
 
 def encode(value, inverse):
@@ -134,7 +154,7 @@
     return value * jnp.abs(value) * scale
 
 
-def reduce_kernel(q_ref, m_ref, out_ref, acc, snd, rcv, s_m, r_m, m_snd, m_rcv, send_sem, recv_sem, sm_send, sm_recv, mir_send, mir_recv, *, n, nb, width, mirrored):
+def reduce_kernel(first_ref, q_ref, m_ref, out_ref, acc, snd, rcv, s_m, r_m, m_snd, m_rcv, send_sem, recv_sem, sm_send, sm_recv, mir_send, mir_recv, *, n, nb, width, mirrored):
     chunks, _, rows, cw = q_ref.shape
     size = out_ref.shape[1] // nb
     per = width // chunks
@@ -165,7 +185,7 @@
     def data_copy(k, c):
         span = pl.ds(starts[k], counts[k])
         return pltpu.make_async_remote_copy(
-            src_ref=snd.at[c, span], dst_ref=rcv.at[c, span], send_sem=send_sem.at[k, c], recv_sem=recv_sem.at[k, c],
+            src_ref=snd.at[c, span] if k else first_ref.at[c], dst_ref=rcv.at[c, span], send_sem=send_sem.at[k, c], recv_sem=recv_sem.at[k, c],
             device_id={"aux": partner[k]}, device_id_type=MESH)
 
     def mirror_copy(d):
@@ -177,19 +197,13 @@
         out_ref[:, pl.ds(pl.multiple_of(block * size, size), size)] = value
 
     def before(k, c, j):
-        return q_ref[c, pl.ds(bit[0] * counts[0] + j, steps[k])] if k == 1 else acc[c, pl.ds(j, steps[k])]
+        return q_ref[c, pl.ds(j, steps[k])] if k == 1 else acc[c, pl.ds(j, steps[k])]
 
     def event(k, c):
         if k == 0:
             if c == 0:
-                s_m[0] = jnp.maximum(m_ref[...], TINY)
+                s_m[0] = m_ref[...]
                 scale_copy(0).start()
-            inverse = 1.0 / s_m[0, 0:1]
-
-            @pl.loop(0, counts[0], step=steps[0])
-            def _(j):
-                snd[c, pl.ds(j, steps[0])] = encode(q_ref[c, pl.ds((1 - bit[0]) * counts[0] + j, steps[0])], inverse)
-
             data_copy(0, c).start()
             return
         if c == 0:
@@ -249,7 +263,6 @@
     width = nb // 2 + 1 if mirrored else nb
     per = 1 if mirrored else 2
     chunks, cw, rows = width // per, per * size, size // split
-    bits = nb.bit_length() - 1
     stages = n.bit_length() - 1
     gathered = pl.pallas_call(
         functools.partial(gather_kernel, n=n),
@@ -260,17 +273,24 @@
         compiler_params=pltpu.CompilerParams(collective_id=1, has_side_effects=True, vmem_limit_bytes=VMEM_BYTES),
     )(coeffs.T).reshape(nb, size, LANES)
 
-    q, m = pl.pallas_call(
-        functools.partial(slab_kernel, slots=slots, width=width, split=split),
+    batch = nb // 4
+    parts = max(split // 2, 1)
+    shape = (chunks, parts, nb // 2 if split == 1 else nb, rows, cw)
+    turns = nb // 2 // batch if split == 1 else nb // batch
+    block = (chunks, parts, batch, rows, cw)
+    late = turns if split == 1 else 0
+    send, keep, m = pl.pallas_call(
+        functools.partial(slab_kernel, width=width, split=split),
         grid_spec=pltpu.PrefetchScalarGridSpec(
             num_scalar_prefetch=3,
-            grid=(slots + nb,),
+            grid=(nb // batch,),
             in_specs=[
-                pl.BlockSpec((1, aux, size, size), lambda g, *_: (jnp.minimum(g, slots - 1), 0, 0, 0)),
-                pl.BlockSpec((nb, size, LANES), lambda g, *_: (0, 0, 0)),
+                pl.BlockSpec(three_index.shape, lambda g, *_: (0, 0, 0, 0), pipeline_mode=pl.Buffered(1)),
+                pl.BlockSpec((nb, size, LANES), lambda g, *_: (0, 0, 0), pipeline_mode=pl.Buffered(1)),
             ],
             out_specs=[
-                pl.BlockSpec((chunks, split, 1, rows, cw), lambda g, *_: (0, 0, flip(jnp.maximum(g - slots, 0), bits), 0, 0)),
+                pl.BlockSpec(block, lambda g, *_: (0, 0, jnp.minimum(g, turns - 1), 0, 0)),
+                pl.BlockSpec(block, lambda g, *_: (0, 0, jnp.maximum(g - late, 0), 0, 0)),
                 pl.BlockSpec((8, cw), lambda g, *_: (0, 0)),
             ],
             scratch_shapes=[
@@ -280,7 +300,8 @@
             ],
         ),
         out_shape=[
-            jax.ShapeDtypeStruct((chunks, split, nb, rows, cw), jnp.float32),
+            jax.ShapeDtypeStruct(shape, jnp.int16),
+            jax.ShapeDtypeStruct(shape, jnp.float32),
             jax.ShapeDtypeStruct((8, cw), jnp.float32),
         ],
         compiler_params=pltpu.CompilerParams(vmem_limit_bytes=VMEM_BYTES, dimension_semantics=("arbitrary",)),
@@ -289,7 +310,7 @@
     return pl.pallas_call(
         functools.partial(reduce_kernel, n=n, nb=nb, width=width, mirrored=mirrored),
         out_shape=jax.ShapeDtypeStruct((rows, nb * size), jnp.float32),
-        in_specs=[pl.BlockSpec(memory_space=pltpu.VMEM)] * 2,
+        in_specs=[pl.BlockSpec(memory_space=pltpu.VMEM)] * 3,
         out_specs=pl.BlockSpec(memory_space=pltpu.VMEM),
         scratch_shapes=[
             pltpu.VMEM((chunks, n // 4, rows, cw), jnp.float32),
@@ -307,7 +328,7 @@
             pltpu.SemaphoreType.DMA((width,)),
         ],
         compiler_params=pltpu.CompilerParams(collective_id=0, has_side_effects=True, vmem_limit_bytes=VMEM_BYTES),
-    )(q.reshape(chunks, n, rows, cw), m)
+    )(send.reshape(chunks, n // 2, rows, cw), keep.reshape(chunks, n // 2, rows, cw), m)
 
 
 def solution(mesh):

time: 114 us -> 110 us (0.965)
  Pallas kernels: 111 us -> 108 us
    pallas_call x1, Pallas kernels: 19.3 us -> 14.9 us  [per_device(): pl.pallas_call(functools.partial(slab_kernel, width=width, split=split),...]
where the time goes in v1:
time: 110 us; the launch traced here: 111 us
  Pallas kernels  108 us (98%)
  local copies, waits for them, and re-layouts  2.3 us (2%)
    pallas_call x1, Pallas kernels, per_device(): pl.pallas_call(functools.partial(reduce_kernel, n=n, nb=nb, width=width,...  74.5 us
    pallas_call x1, Pallas kernels, per_device(): pl.pallas_call(functools.partial(gather_kernel, n=n), out_shape=jax.Shape...  18.4 us
    pallas_call x1, Pallas kernels, per_device(): pl.pallas_call(functools.partial(slab_kernel, width=width, split=split),...  14.9 us
    unnamed x1, local copies, waits for them, and re-layouts  2.3 us

profile of v1, /device:TPU:1, one launch (start us, length us, event | category | flops | bytes accessed | tf_op | source)
XLA Modules:
  0.0 110.8 jit_solution(9219544862030612895)
XLA Ops:
  0.7 18.4 %shard_map.55.c_ref = bf16[16,128,256]{2,1,0:T(8,128)(2,1)} custom-call(bf16[200,128]{1,0:T(8,128)(2,1)} %bitcast.5), custom_call_target="tpu_custom_call" | custom-call | tf_op jit(solution)/shard_map/pallas_call | solution.py:267
  19.0 14.9 %shard_map.56 = (s16[9,1,8,128,128]{4,3,2,1,0:T(8,128)(2,1)}, f32[9,1,8,128,128]{4,3,2,1,0:T(8,128)}, f32[8,128]{1,0:T(8,128)}) custom-call(s32[16]{0:T(128)} %blocks.1, s32[1]{0:T(128)S(6)} %copy.7.count, s32[16,16]{1,0:T(8,128)} %mask.1, bf16[16,8,128,128]{3,2,1,0:T(8,128)(2,1)} %t_ref.1, bf16[16,128,256]{2,1,0:T(8,128)(2,1)} %shard_map.55.c_ref), custom_call_target="tpu_custom_call" | custom-call | tf_op jit(solution)/shard_map/pallas_call | solution.py:282
  34.0 74.5 %shard_map.57 = f32[128,2048]{1,0:T(8,128)} custom-call(s16[9,8,128,128]{3,2,1,0:T(8,128)(2,1)} %bitcast.4, f32[9,8,128,128]{3,2,1,0:T(8,128)} %bitcast.3, f32[8,128]{1,0:T(8,128)} %get-tuple-element.10.m_ref), custom_call_target="tpu_custom_call" | custom-call | tf_op jit(solution)/shard_map/pallas_call | solution.py:310
  108.5 2.3 %copy.8 = f32[128,2048]{1,0:T(8,128)} copy(f32[128,2048]{1,0:T(8,128)} %shard_map.57) | data formatting | bytes 2097152

commit v2 on v1

--- a/solution.py
+++ b/solution.py
@@ -10,7 +10,7 @@
 MESH = pl.DeviceIdType.MESH
 VMEM_BYTES = 56 * 1024 * 1024
 TOP = 32000.0
-TINY = 1e-37
+TINY = 1e-28
 LANES = 256
 
 
@@ -145,8 +145,9 @@
 
 
 def encode(value, inverse):
-    root = jnp.sqrt(jnp.abs(value) * inverse) * TOP + 0.5
-    return jnp.where(value < 0, -root, root).astype(jnp.int16)
+    scaled = value * (inverse * (TOP * TOP))
+    root = scaled * lax.rsqrt(jnp.abs(scaled) + 1e-20)
+    return (root + jnp.where(scaled < 0, -0.5, 0.5)).astype(jnp.int16)
 
 
 def decode(code, scale):

time: 110 us -> 112 us (1.018); the launches traced: 111 us -> 111 us
    pallas_call x1, Pallas kernels: 74.5 us -> 69.9 us  [per_device(): pl.pallas_call(functools.partial(reduce_kernel, n=n, nb=nb, width=width,...]
    pallas_call x1, Pallas kernels: 14.9 us -> 19.5 us  [per_device(): pl.pallas_call(functools.partial(slab_kernel, width=width, split=split),...]
where the time goes in v2:
time: 112 us; the launch traced here: 111 us
  Pallas kernels  108 us (96%)
  local copies, waits for them, and re-layouts  2.3 us (2%)
    pallas_call x1, Pallas kernels, per_device(): pl.pallas_call(functools.partial(reduce_kernel, n=n, nb=nb, width=width,...  69.9 us
    pallas_call x1, Pallas kernels, per_device(): pl.pallas_call(functools.partial(slab_kernel, width=width, split=split),...  19.5 us
    pallas_call x1, Pallas kernels, per_device(): pl.pallas_call(functools.partial(gather_kernel, n=n), out_shape=jax.Shape...  18.4 us
    unnamed x1, local copies, waits for them, and re-layouts  2.3 us

profile of v2, /device:TPU:1, one launch (start us, length us, event | category | flops | bytes accessed | tf_op | source)
XLA Modules:
  0.0 110.7 jit_solution(16212328445519908986)
XLA Ops:
  0.7 18.4 %shard_map.55.c_ref = bf16[16,128,256]{2,1,0:T(8,128)(2,1)} custom-call(bf16[200,128]{1,0:T(8,128)(2,1)} %bitcast.5), custom_call_target="tpu_custom_call" | custom-call | tf_op jit(solution)/shard_map/pallas_call | solution.py:268
  19.0 19.5 %shard_map.56 = (s16[9,1,8,128,128]{4,3,2,1,0:T(8,128)(2,1)}, f32[9,1,8,128,128]{4,3,2,1,0:T(8,128)}, f32[8,128]{1,0:T(8,128)}) custom-call(s32[16]{0:T(128)} %blocks.1, s32[1]{0:T(128)S(6)} %copy.7.count, s32[16,16]{1,0:T(8,128)} %mask.1, bf16[16,8,128,128]{3,2,1,0:T(8,128)(2,1)} %t_ref.1, bf16[16,128,256]{2,1,0:T(8,128)(2,1)} %shard_map.55.c_ref), custom_call_target="tpu_custom_call" | custom-call | tf_op jit(solution)/shard_map/pallas_call | solution.py:283
  38.5 69.9 %shard_map.57 = f32[128,2048]{1,0:T(8,128)} custom-call(s16[9,8,128,128]{3,2,1,0:T(8,128)(2,1)} %bitcast.4, f32[9,8,128,128]{3,2,1,0:T(8,128)} %bitcast.3, f32[8,128]{1,0:T(8,128)} %get-tuple-element.10.m_ref), custom_call_target="tpu_custom_call" | custom-call | tf_op jit(solution)/shard_map/pallas_call | solution.py:311
  108.4 2.3 %copy.8 = f32[128,2048]{1,0:T(8,128)} copy(f32[128,2048]{1,0:T(8,128)} %shard_map.57) | data formatting | bytes 2097152

commit v3 on v2

--- a/solution.py
+++ b/solution.py
@@ -56,7 +56,7 @@
     nb, size, _ = c_ref.shape
     slots, aux = t_ref.shape[:2]
     chunks, parts, batch, rows, cw = send_ref.shape
-    group = max(d for d in range(1, 5) if width % d == 0)
+    group = max(d for d in range(1, 10) if width % d == 0)
     per = cw // size
     mine = lax.axis_index("aux") % 2
 

time: 112 us -> 110 us (0.982)
    pallas_call x1, Pallas kernels: 19.5 us -> 10.6 us  [per_device(): pl.pallas_call(functools.partial(slab_kernel, width=width, split=split),...]
    pallas_call x1, Pallas kernels: 69.9 us -> 77.8 us  [per_device(): pl.pallas_call(functools.partial(reduce_kernel, n=n, nb=nb, width=width,...]
where the time goes in v3:
time: 110 us
  Pallas kernels  107 us (97%)
  local copies, waits for them, and re-layouts  2.3 us (2%)
    pallas_call x1, Pallas kernels, per_device(): pl.pallas_call(functools.partial(reduce_kernel, n=n, nb=nb, width=width,...  77.8 us
    pallas_call x1, Pallas kernels, per_device(): pl.pallas_call(functools.partial(gather_kernel, n=n), out_shape=jax.Shape...  18.4 us
    pallas_call x1, Pallas kernels, per_device(): pl.pallas_call(functools.partial(slab_kernel, width=width, split=split),...  10.6 us
    unnamed x1, local copies, waits for them, and re-layouts  2.3 us

profile of v3, /device:TPU:1, one launch (start us, length us, event | category | flops | bytes accessed | tf_op | source)
XLA Modules:
  0.0 109.7 jit_solution(5201565233254650318)
XLA Ops:
  0.7 18.4 %shard_map.55.c_ref = bf16[16,128,256]{2,1,0:T(8,128)(2,1)} custom-call(bf16[200,128]{1,0:T(8,128)(2,1)} %bitcast.5), custom_call_target="tpu_custom_call" | custom-call | tf_op jit(solution)/shard_map/pallas_call | solution.py:268
  19.0 10.6 %shard_map.56 = (s16[9,1,8,128,128]{4,3,2,1,0:T(8,128)(2,1)}, f32[9,1,8,128,128]{4,3,2,1,0:T(8,128)}, f32[8,128]{1,0:T(8,128)}) custom-call(s32[16]{0:T(128)} %blocks.1, s32[1]{0:T(128)S(6)} %copy.7.count, s32[16,16]{1,0:T(8,128)} %mask.1, bf16[16,8,128,128]{3,2,1,0:T(8,128)(2,1)} %t_ref.1, bf16[16,128,256]{2,1,0:T(8,128)(2,1)} %shard_map.55.c_ref), custom_call_target="tpu_custom_call" | custom-call | tf_op jit(solution)/shard_map/pallas_call | solution.py:283
  29.6 77.8 %shard_map.57 = f32[128,2048]{1,0:T(8,128)} custom-call(s16[9,8,128,128]{3,2,1,0:T(8,128)(2,1)} %bitcast.4, f32[9,8,128,128]{3,2,1,0:T(8,128)} %bitcast.3, f32[8,128]{1,0:T(8,128)} %get-tuple-element.10.m_ref), custom_call_target="tpu_custom_call" | custom-call | tf_op jit(solution)/shard_map/pallas_call | solution.py:311
  107.4 2.3 %copy.8 = f32[128,2048]{1,0:T(8,128)} copy(f32[128,2048]{1,0:T(8,128)} %shard_map.57) | data formatting | bytes 2097152
